TPU v7x, 32 devices: a whole 2x2x4 slice. The times are simulated.
32 devices in a mesh: groups: 2 (over y), row: 4 (over z), col: 4 (over x, core).
Axes of the slice: x: 2, y: 2, z: 4, core: 2. Of those that a mesh axis runs over, the one named last changes fastest.
Arguments:
- positions: float32 [4096, 3, 128], P(('groups', 'row', 'col')), parts along dimension 0, may hold values from -6 to 6
- normals: float32 [4096, 3, 128], P(('groups', 'row', 'col')), parts along dimension 0, may hold values from -6 to 6
- curvature: float32 [4096, 128], P(('groups', 'row', 'col')), parts along dimension 0, may hold values from 0.5 to 3
- pair_targets: int32 [32, 512], P(('groups', 'row', 'col')), parts along dimension 0, may hold values from 0 to 511, as said below
- pair_sources: int32 [32, 512], P(('groups', 'row', 'col')), parts along dimension 0, may hold values from 0 to 511
- pair_count: int32 [32], P(('groups', 'row', 'col')), parts along dimension 0, may hold values from 64 to 512, as said below
- node_counts: int32 [512, 8], P('groups'), parts along dimension 0, may hold values from 1 to 128, 642 in all within a row
- drop_clusters: int32 [512, 8], P('groups'), parts along dimension 0, may hold values from 0 to 2047, as said below
- drop_owner: int32 [512], P('groups'), parts along dimension 0, may hold values from 0 to 15, as said below
Outputs:
- drop_velocity: float32 [4096, 3, 128], P(('groups', 'row', 'col')), parts along dimension 0
There are 2 independent parts, one for each index of `groups`. A program takes and returns all parts, laid end to end along the dimension named above; each array names one. Nothing has to cross between parts.
Inputs may be any that keep to these rules, and one draw needn't show every extreme that they name: `drop_clusters`: every cluster of 0 to 2047 appears exactly once. Of the 128 clusters of one device, at most 16 belong to drops of any one owner, and this many is reached. `drop_owner`: every device owns exactly 16 drops. `pair_count`: the largest count is reached on some device; list entries past a device's count are not pairs. In each device's list, at most 256 entries have the same value of pair_targets // 128, and every device's list reaches this many for some value. `node_counts`: each drop's counts sum to 642.
All inputs are finite; a program needn't handle non-finite values.
Results may differ from a plain program's by a relative error of at most 0.0003.
Values sent between devices are 32-bit elements; how exact they have to be, the bound alone decides.
No kernel may reach another device: no remote copies, remote signals or barrier semaphores. Data moves between devices by JAX's collectives and lax.ppermute only.
A program may use at most 64 MiB of HBM per device.

v0:
```python
import functools
import math

import jax
import jax.numpy as jnp
from jax import lax
from jax.experimental import pallas as pl
from jax.experimental.pallas import tpu as pltpu
from jax.sharding import PartitionSpec as P

f32 = jnp.float32
bf16 = jnp.bfloat16
i32 = jnp.int32
regular_sq = 0.0025
length_scale = 1.0 / math.sqrt(regular_sq)
force_scale = length_scale / (8.0 * math.pi)
unroll = 8
levels = 2
vmem_limit = 24 * 2**20
kernel_flops = 8 * 10**9
whole_vmem = 60 * 2**20
vmem = pl.BlockSpec(memory_space=pltpu.VMEM)
smem = pl.BlockSpec(memory_space=pltpu.SMEM)
hbm = pl.BlockSpec(memory_space=pltpu.HBM)


def split3(value):
    high = value.astype(bf16)
    rest = value - high.astype(f32)
    mid = rest.astype(bf16)
    low = (rest - mid.astype(f32)).astype(bf16)
    return high.astype(f32), mid.astype(f32), low.astype(f32)


def rows16(upper, lower):
    return jnp.concatenate([upper, lower], axis=0).astype(bf16)


def transposed_left(y, f, slots):
    row = lax.broadcasted_iota(i32, (8, slots), 0)
    dot = -(y[0] * f[0] + y[1] * f[1] + y[2] * f[2])
    tile = jnp.where(row == 7, dot, 0.0)
    for k in range(3):
        tile = jnp.where(row == k, y[k], jnp.where(row == 3 + k, f[k], tile))
    high, mid, low = split3(tile)
    first = row < 3
    high_one = jnp.where(first, 1.0, high)
    left = jnp.concatenate(
        [rows16(high, mid), rows16(low, high_one), rows16(high_one, jnp.where(first, 1.0, mid))], axis=0
    )
    return left.T


def products(left, x, slots):
    row = lax.broadcasted_iota(i32, (8, slots), 0)
    zero = jnp.zeros((8, slots), f32)
    tile = jnp.where(row == 7, 1.0, zero)
    for k in range(3):
        tile = jnp.where((row == k) | (row == 3 + k), x[k], tile)
    high, mid, low = split3(tile)
    columns = []
    for k in range(3):
        mine = row == k
        minus = jnp.where(mine, -1.0, zero)
        columns.append(
            [
                rows16(minus, minus),
                rows16(minus, jnp.where(mine, high, 0.0)),
                rows16(jnp.where(mine, mid, 0.0), jnp.where(mine, low, 0.0)),
            ]
        )
    first = row < 3
    high, mid, low = [jnp.where(first, 0.0, part) for part in (high, mid, low)]
    columns.append([rows16(high, high), rows16(high, mid), rows16(low, mid)])
    for k in range(2):
        pick = jnp.where(row == 3 + k, 1.0, zero)
        columns.append([rows16(pick, pick), rows16(pick, zero), rows16(zero, zero)])
    right = jnp.concatenate([jnp.concatenate(column, axis=0) for column in columns], axis=1)
    return lax.dot_general(left, right, (((1,), (0,)), ((), ())), preferred_element_type=f32)


def node_sums(product, force_z, slots):
    row = lax.broadcasted_iota(i32, (8, slots), 0)
    total = None
    for g in range(product.shape[0] // 8):
        part = product[8 * g : 8 * g + 8]
        wx, wy, wz, dot, fx, fy = [part[:, slots * k : slots * (k + 1)] for k in range(6)]
        fz = force_z[8 * g : 8 * g + 8]
        inverse = lax.rsqrt(wx * wx + wy * wy + (wz * wz + 1.0))
        cube = inverse * inverse * inverse
        isotropic = inverse + cube
        project = dot * cube
        terms = (isotropic * fx + project * wx, isotropic * fy + project * wy, isotropic * fz + project * wz)
        total = terms if total is None else tuple(a + b for a, b in zip(total, terms))
    sums = [jnp.broadcast_to(jnp.sum(part, axis=0, keepdims=True), (8, slots)) for part in total]
    return jnp.where(row == 0, sums[0], jnp.where(row == 1, sums[1], jnp.where(row == 2, sums[2], 0.0)))


def hop_kernel(spec, list_ref, mate_list_ref, *refs):
    n, slots, hop, homes, own, mate, first, emit, split = spec
    refs = list(refs)
    if first:
        target_refs = [refs.pop(0) for _ in range(homes)]
    else:
        target_ref, _, _ = refs.pop(0), refs.pop(0), refs.pop(0)
    own_refs = [refs.pop(0) for _ in range(own)]
    mate_refs = [refs.pop(0) for _ in range(mate)]
    if first:
        total_ref, token_ref, target_ref = refs.pop(0), refs.pop(0), refs.pop(0)
    else:
        total_ref, token_ref = refs.pop(0), refs.pop(0)
        out_refs = [refs.pop(0) for _ in emit]
    source_ref, left_ref = refs
    token_ref[...] = jnp.zeros_like(token_ref)
    clusters = homes * n
    shift = n.bit_length() - 1
    if first:
        for h in range(homes):
            target_ref[3 * n * h : 3 * n * (h + 1), :] = target_refs[h][: 3 * n, :]
        total_ref[...] = jnp.zeros_like(total_ref)
    for place, block in list(enumerate(own_refs)) + [(2 + b, block) for b, block in enumerate(mate_refs)]:
        source_ref[6 * n * place : 6 * n * (place + 1), :] = block[...]

    bound_row = list_ref.shape[0] - 1

    def wide(value):
        return jnp.broadcast_to(value, (8, slots))

    def run(level):
        groups = slots // 8 * (levels - level) // levels
        lane = hop * levels + level
        own_start, own_end = list_ref[bound_row, lane], list_ref[bound_row, lane + 1]
        mate_start, mate_end = mate_list_ref[bound_row, lane], mate_list_ref[bound_row, lane + 1]
        own_count = (own_end - own_start + 1) >> 1
        count = own_count + ((mate_end - mate_start) >> 1)
        after_own = mate_start + 1 - 2 * own_count

        def entry(index):
            live = index < count
            mine = index < own_count
            place = jnp.where(live, 2 * index + jnp.where(mine, own_start, after_own), 0)
            row, column_of = place >> 7, place & 127
            packed = jnp.where(mine, list_ref[row, column_of], mate_list_ref[row, column_of])
            packed = jnp.where(live, packed, 0)
            target = (packed & 0xFFF) ^ jnp.where(mine, 0, n if split else 0)
            source = (packed >> 12) + jnp.where(mine, 0, 2 * n)
            return live, target, jnp.where(live, source, 0)

        def fetch(index, u):
            _, _, source = entry(index)
            base = source + (source >> shift) * (5 * n)
            values = [wide(source_ref[pl.ds(base + n * k, 1), :]) for k in range(6)]
            left_ref[u] = transposed_left(values[:3], values[3:], slots)

        @pl.when(count > 0)
        def _():
            for u in range(unroll):
                fetch(u, u)

        def step(i, carry):
            results = []
            lefts = [left_ref[u, : 8 * groups] for u in range(unroll)]
            for u in range(unroll):
                live, target, source = entry(i * unroll + u)
                base = target + (target >> shift) * (2 * n)
                x = [wide(target_ref[pl.ds(base + n * k, 1), :]) for k in range(3)]
                product = products(lefts[u], x, slots)
                force_z = source_ref[pl.ds(source + (source >> shift) * (5 * n) + 5 * n, 1), :]
                force_z = jnp.broadcast_to(force_z, (slots, slots)).T
                results.append((jnp.where(live, target, clusters), node_sums(product, force_z, slots)))
            for u in range(unroll):
                fetch((i + 1) * unroll + u, u)
            for target, result in results:
                total_ref[pl.ds(target * 4, 4), :] += result[:4]
            return carry

        lax.fori_loop(0, (count + unroll - 1) // unroll, step, 0)

    for level in range(levels):
        run(level)
    for out_ref, out_homes in zip(out_refs if emit else [], emit):
        for place, h in enumerate(out_homes):

            def move(i, carry, h=h, out_ref=out_ref, first_row=3 * n * place):
                for u in range(8):
                    tile = total_ref[pl.ds((n * h + i * 8 + u) * 4, 4), :]
                    out_ref[pl.ds(first_row + i * 24 + 3 * u, 3), :] = tile[:3]
                return carry

            lax.fori_loop(0, n // 8, move, 0)


def hop_call(n, hop, emit, lists, targets, token, total, own, mate, split):
    first = hop == 0
    slots = own[0].shape[1]
    homes = len(targets) if first else targets[0].shape[0] // (3 * n)
    total_shape = jax.ShapeDtypeStruct((homes * n * 4 + 8, slots), f32)
    aliases = {}
    operands = [*lists, *targets]
    if not first:
        operands += [token, total]
    out_shape = [total_shape, jax.ShapeDtypeStruct((8, 128), f32)]
    if first:
        out_shape += [jax.ShapeDtypeStruct((homes * 3 * n, slots), f32)]
    out_shape += [jax.ShapeDtypeStruct((len(out_homes) * 3 * n, slots), f32) for out_homes in emit]
    if not first:
        aliases = {len(operands) - 1: 0}
    operands += [*own, *mate]
    spec = (n, slots, hop, homes, len(own), len(mate), first, emit, split)
    return pl.pallas_call(
        functools.partial(hop_kernel, spec),
        out_shape=out_shape,
        in_specs=[smem, smem] + [vmem] * (len(operands) - 2),
        out_specs=[vmem] * len(out_shape),
        scratch_shapes=[
            pltpu.VMEM((4 * 6 * n, slots), f32),
            pltpu.VMEM((unroll, slots, 48), bf16),
        ],
        input_output_aliases=aliases,
        compiler_params=pltpu.CompilerParams(vmem_limit_bytes=vmem_limit),
        cost_estimate=pl.CostEstimate(flops=kernel_flops if hop else kernel_flops // 8, bytes_accessed=10**6, transcendentals=10**6),
        name=f"pairs_hop{hop}",
    )(*operands)


def column(row, rows):
    return jnp.broadcast_to(row, (rows, 128)).T


def prep_kernel(n, base_ref, *refs):
    ins, (out_ref, own_ref, small_ref), held, sems = refs[:8], refs[8:11], refs[11:19], refs[19]
    copies = [pltpu.make_async_copy(a, b, sems.at[k]) for k, (a, b) in enumerate(zip(ins, held))]
    for copy in copies:
        copy.start()
    for copy in copies:
        copy.wait()
    position_ref, normal_ref, curvature_ref, cluster_ref, count_ref, owner_ref, target_ref, source_ref = held
    slots = position_ref.shape[1]
    scaled = position_ref[...] * length_scale
    out_ref[: 3 * n, :] = scaled
    own_ref[...] = scaled
    mine = base_ref[0] + lax.broadcasted_iota(i32, (n, 128), 0)
    total = jnp.zeros((n, 128), f32)
    for k in range(cluster_ref.shape[0]):
        for j in range(cluster_ref.shape[1] // 128):
            part = slice(128 * j, 128 * (j + 1))
            cluster = jnp.broadcast_to(cluster_ref[k : k + 1, part], (n, 128))
            count = jnp.broadcast_to(count_ref[k : k + 1, part].astype(f32), (n, 128))
            total = total + jnp.where(cluster == mine, count, 0.0)
    live_count = jnp.sum(total, axis=1, keepdims=True)
    lane = lax.broadcasted_iota(i32, (n, slots), 1).astype(f32)
    strength = jnp.where(lane < live_count, curvature_ref[...] * force_scale, 0.0)
    for k in range(3):
        out_ref[n * (3 + k) : n * (4 + k), :] = normal_ref[n * k : n * (k + 1), :] * strength
    per_drop, drops = cluster_ref.shape
    pairs = target_ref.shape[1]
    small_ref[:per_drop, :drops] = cluster_ref[...] + (count_ref[...] << 14)
    small_ref[per_drop : per_drop + 1, :drops] = owner_ref[...]
    small_ref[per_drop + 1 : per_drop + 2, :pairs] = target_ref[...]
    small_ref[per_drop + 2 : per_drop + 3, :pairs] = source_ref[...]


def prep_call(base, *operands):
    n, slots = operands[2].shape
    per_drop, drops = operands[3].shape
    small = (per_drop + 8, max(drops, operands[6].shape[1]))
    shapes = [((6 * n, slots), f32), ((3 * n, slots), f32), (small, i32)]
    return pl.pallas_call(
        functools.partial(prep_kernel, n),
        out_shape=[jax.ShapeDtypeStruct(*shape) for shape in shapes],
        in_specs=[smem] + [hbm] * 8,
        out_specs=[vmem] * 3,
        scratch_shapes=[pltpu.VMEM(x.shape, x.dtype) for x in operands] + [pltpu.SemaphoreType.DMA((8,))],
        compiler_params=pltpu.CompilerParams(vmem_limit_bytes=whole_vmem),
        name="prep_sources",
    )(base, *operands)


def index_kernel(spec, facts_ref, *refs):
    n, rows, cols, capacity, per_drop, drops, pair_slots, split = spec
    small_ref, list_ref, place_ref = refs
    my_row, my_col, device, live_pairs = [facts_ref[k] for k in range(4)]
    shift = n.bit_length() - 1
    wide = (128, 128)
    lane_row = lax.broadcasted_iota(i32, (1, 128), 1)
    sub = lax.broadcasted_iota(i32, wide, 0)
    lane = lax.broadcasted_iota(i32, wide, 1)

    blocks = pair_slots // 128
    wide_source = []
    for b in range(blocks):
        source = small_ref[per_drop + 2 : per_drop + 3, 128 * b : 128 * (b + 1)]
        cluster = ((source >> shift) * cols + my_col) * n + (source & (n - 1))
        wide_source.append(jnp.broadcast_to(cluster, wide))

    def look_up(j, counts):
        part = pl.ds(pl.multiple_of(j * 128, 128), 128)
        for k in range(per_drop):
            fact = column(small_ref[k : k + 1, part], 128)
            cluster, count = fact & 16383, (fact >> 14).astype(f32)
            counts = [c + jnp.where(cluster == w, count, 0.0) for c, w in zip(counts, wide_source)]
        return counts

    counts = lax.fori_loop(0, drops // 128, look_up, [jnp.zeros(wide, f32)] * blocks)
    keys, packs = [], []
    for b in range(blocks):
        target = small_ref[per_drop + 1 : per_drop + 2, 128 * b : 128 * (b + 1)]
        source = small_ref[per_drop + 2 : per_drop + 3, 128 * b : 128 * (b + 1)]
        ahead = ((source >> shift) - my_row) & (rows - 1)
        hop = jnp.minimum(ahead, rows - ahead)
        index = lane_row + 128 * b
        if split:
            hop = jnp.where((hop == rows // 2) & (((target >> shift) ^ my_col) < 2), hop + 1, hop)
        key = jnp.where(index < live_pairs, hop, rows)
        count = jnp.sum(counts[b], axis=0, keepdims=True)
        level = jnp.zeros((1, 128), i32)
        for k in range(1, levels):
            level = level + jnp.where(count <= n * k / levels, 1, 0)
        keys.append((key * levels + level) * (128 * blocks) + index)
        home = target >> shift
        if split:
            home = home ^ my_col
        side = jnp.where((ahead > 0) & (ahead * 2 < rows), n, 0)
        packs.append((home * n + (target & (n - 1)) + (side + (source & (n - 1))) * 4096).astype(f32))
    key_columns = [column(key, 128) for key in keys]
    order_columns = []
    for b in range(blocks):
        before = jnp.zeros(wide, f32)
        for c in range(blocks):
            before = before + jnp.where(key_columns[c] < jnp.broadcast_to(keys[b], wide), 1.0, 0.0)
        order_columns.append(column(jnp.sum(before, axis=0, keepdims=True), 128))
    pack_columns = [column(pack, 128) for pack in packs]
    lanes = lane.astype(f32)
    for b in range(blocks):
        ordered = jnp.zeros(wide, f32)
        for c in range(blocks):
            ordered = ordered + jnp.where(order_columns[c] == lanes + 128.0 * b, pack_columns[c], 0.0)
        list_ref[b : b + 1, :] = jnp.sum(ordered, axis=0, keepdims=True).astype(i32)
    below = jnp.zeros(wide, f32)
    for c in range(blocks):
        below = below + jnp.where(key_columns[c] < lane * (128 * blocks), 1.0, 0.0)
    list_ref[blocks : blocks + 1, :] = jnp.sum(below, axis=0, keepdims=True).astype(i32)

    mine = device * n + sub

    def scan(j, carry):
        owner_sum, chosen, owned_before = carry
        part = pl.ds(pl.multiple_of(j * 128, 128), 128)
        owner = small_ref[per_drop : per_drop + 1, part]
        is_mine = jnp.where(owner == device, 1.0, 0.0)
        mine_column = column(is_mine, 128)
        rank = jnp.sum(jnp.where(sub < lane, mine_column, 0.0), axis=0, keepdims=True) + owned_before
        slot = jnp.where(owner == device, rank, -1.0)
        picked = column(slot, 128) == (lane // per_drop).astype(f32)
        for k in range(per_drop):
            fact = small_ref[k : k + 1, part]
            cluster = fact & 16383
            chosen = chosen + jnp.where(picked & (lane % per_drop == k), column(fact.astype(f32), 128), 0.0)
            wide_owner = jnp.broadcast_to(owner.astype(f32), wide)
            owner_sum = owner_sum + jnp.where(jnp.broadcast_to(cluster, wide) == mine, wide_owner, 0.0)
        return owner_sum, chosen, owned_before + jnp.sum(is_mine, axis=1, keepdims=True)

    start = (jnp.zeros(wide, f32), jnp.zeros(wide, f32), jnp.zeros((1, 1), f32))
    owner_sum, chosen, _ = lax.fori_loop(0, drops // 128, scan, start)
    home_owner = jnp.broadcast_to(jnp.sum(owner_sum, axis=1, keepdims=True), wide)
    owner_lanes = home_owner.T
    rank = jnp.sum(jnp.where((home_owner == owner_lanes) & (sub < lane), 1.0, 0.0), axis=0, keepdims=True)
    place_ref[0:1, :] = ((owner_lanes[0:1] * capacity + rank) * 3.0).astype(i32)
    fact = jnp.sum(chosen, axis=0, keepdims=True).astype(i32)
    cluster = fact & 16383
    anchor = cluster >> shift
    cluster_column = column(cluster, 128)
    cluster_wide = jnp.broadcast_to(cluster, wide)
    same = (cluster_column >> shift) == (cluster_wide >> shift)
    rank = jnp.sum(jnp.where(same & (cluster_column < cluster_wide), 1.0, 0.0), axis=0, keepdims=True)
    place_ref[1:2, :] = (anchor * capacity + rank.astype(i32)) * 3
    place_ref[2:3, :] = fact >> 14


def index_call(spec, facts, small):
    return pl.pallas_call(
        functools.partial(index_kernel, spec),
        out_shape=[jax.ShapeDtypeStruct((spec[6] // 128 + 1, 128), i32), jax.ShapeDtypeStruct((3, 128), i32)],
        in_specs=[smem, vmem],
        out_specs=[vmem, vmem],
        compiler_params=pltpu.CompilerParams(vmem_limit_bytes=vmem_limit),
        name="index_work",
    )(facts, small)


def pack_kernel(n, place_ref, *refs):
    *speed_refs, out_ref, speed_ref = refs
    total = speed_refs[0][: 3 * n, :]
    for part in speed_refs[1:]:
        total = total + part[: 3 * n, :]
    speed_ref[...] = total
    out_ref[...] = jnp.zeros_like(out_ref)

    def step(i, carry):
        for u in range(16):
            cluster = i * 16 + u
            out_ref[pl.ds(place_ref[0, cluster], 3), :] = speed_ref[pl.ds(3 * cluster, 3), :]
        return carry

    lax.fori_loop(0, n // 16, step, 0)


def pack_call(places, speeds, n, capacity, devices):
    slots = speeds[0].shape[1]
    return pl.pallas_call(
        functools.partial(pack_kernel, n),
        out_shape=jax.ShapeDtypeStruct((devices * capacity * 3, slots), f32),
        in_specs=[smem] + [vmem] * len(speeds),
        out_specs=vmem,
        scratch_shapes=[pltpu.VMEM((3 * n, slots), f32)],
        compiler_params=pltpu.CompilerParams(vmem_limit_bytes=vmem_limit),
        name="pack_owners",
    )(places, *speeds)


def unpack_kernel(n, place_ref, arrived_ref, out_ref, tile_ref):
    slots = arrived_ref.shape[1]
    lane = lax.broadcasted_iota(i32, (3, slots), 1)

    def step(i, carry):
        for u in range(16):
            cluster = i * 16 + u
            value = arrived_ref[pl.ds(place_ref[1, cluster], 3), :]
            tile_ref[cluster, :3, :] = jnp.where(lane < place_ref[2, cluster], value, 0.0)
        return carry

    lax.fori_loop(0, n // 16, step, 0)
    for k in range(3):
        out_ref[n * k : n * (k + 1), :] = tile_ref[:, k, :]


def unpack_call(places, arrived, n):
    slots = arrived.shape[1]
    return pl.pallas_call(
        functools.partial(unpack_kernel, n),
        out_shape=jax.ShapeDtypeStruct((3 * n, slots), f32),
        in_specs=[smem, vmem],
        out_specs=vmem,
        scratch_shapes=[pltpu.VMEM((n, 8, slots), f32)],
        compiler_params=pltpu.CompilerParams(vmem_limit_bytes=vmem_limit),
        name="unpack_drops",
    )(places, arrived)


def per_device(
    positions,
    normals,
    curvature,
    pair_targets,
    pair_sources,
    pair_count,
    node_counts,
    drop_clusters,
    drop_owner,
):
    n, slots = curvature.shape
    rows = lax.axis_size("row")
    cols = lax.axis_size("col")
    devices = rows * cols
    my_row = lax.axis_index("row")
    my_col = lax.axis_index("col")
    device = my_row * cols + my_col
    capacity = max(2, 2 * n // devices)
    hypercube = cols == 4
    hops = rows // 2 + 1

    def swap(value, bit):
        return lax.ppermute(value, "col", [(c, c ^ bit) for c in range(cols)])

    def component_major(value):
        return jnp.transpose(value, (1, 0, 2)).reshape(3 * n, slots)

    block, position, small = prep_call(
        (device * n).reshape(1),
        component_major(positions),
        component_major(normals),
        curvature,
        drop_clusters.T,
        node_counts.T,
        drop_owner.reshape(1, -1),
        pair_targets,
        pair_sources,
    )
    mate_block = swap(block, 1)
    if hypercube:
        across = swap(position, 2)
    to_right = [(r, (r + 1) % rows) for r in range(rows)]
    to_left = [((r + 1) % rows, r) for r in range(rows)]
    right = lax.ppermute(block, "row", to_right)
    left = lax.ppermute(block, "row", to_left)
    listed, places = index_call(
        (n, rows, cols, capacity, *drop_clusters.shape[::-1], pair_targets.shape[1], hypercube),
        jnp.stack([my_row, my_col, device, pair_count[0]]),
        small,
    )
    if hypercube:
        across, listed = lax.optimization_barrier((across, listed))
        targets = [block, mate_block, across, swap(across, 1)]
    else:
        gathered = lax.all_gather(position, "col", axis=0, tiled=True)
        targets = [gathered[3 * n * h : 3 * n * (h + 1)] for h in range(cols)]
    lists = [listed, swap(listed, 1)]

    total, token, all_targets = hop_call(n, 0, (), lists, targets, None, None, [block], [mate_block], hypercube)
    for hop in range(1, hops):
        if hop + 1 < hops:
            own = [right, left]
        *own, token = lax.optimization_barrier((*own, token))
        mates = [swap(part, 1) for part in own]
        if rows == 4 and hop == 1:
            passed = jnp.where(my_row % 2 == 0, own[0], own[1])
            opposite = [lax.ppermute(passed, "row", [(0, 1), (1, 0), (2, 3), (3, 2)])]
        elif hop + 1 < hops:
            right = lax.ppermute(own[0], "row", to_right)
            left = lax.ppermute(own[1], "row", to_left)
            opposite = [right]
        final = hop + 1 == hops
        emit = () if not final else ((2,), (3,)) if hypercube else (tuple(range(cols)),)
        total, token, *speed = hop_call(n, hop, emit, lists, [all_targets], token, total, own, mates, hypercube)
        if final:
            break
        own = opposite

    if hypercube:
        kept, sent = speed
        crossing, token = lax.optimization_barrier((kept + swap(sent, 1), token))
        across = swap(crossing, 2)
        _, _, kept, sent = hop_call(
            n, hops, ((0,), (1,)), lists, [all_targets], token, total, own, mates, hypercube
        )
        sent, across = lax.optimization_barrier((sent, across))
        home_speed = [kept, swap(sent, 1), across]
    else:
        home_speed = [lax.psum_scatter(speed[0], "col", scatter_dimension=0, tiled=True)]

    outgoing = pack_call(places, home_speed, n, capacity, devices)
    arrived = lax.all_to_all(outgoing, ("row", "col"), split_axis=0, concat_axis=0, tiled=True)
    result = unpack_call(places, arrived, n)
    return jnp.transpose(result.reshape(3, n, slots), (1, 0, 2))


def solution(mesh):
    in_specs = (
        P(("groups", "row", "col"), None, None),
        P(("groups", "row", "col"), None, None),
        P(("groups", "row", "col"), None),
        P(("groups", "row", "col"), None),
        P(("groups", "row", "col"), None),
        P(("groups", "row", "col")),
        P("groups", None),
        P("groups", None),
        P("groups"),
    )
    out_specs = P(("groups", "row", "col"), None, None)
    return jax.shard_map(
        per_device, mesh=mesh, in_specs=in_specs, out_specs=out_specs, check_vma=False
    )
```

profile of v0, /device:TPU:0, one launch (start us, length us, event | category | flops | bytes accessed | tf_op | source)
XLA Modules:
  0.0 77.8 jit_solution(10910352470331838218)
XLA Ops:
  0.0 2.1 %prep_sources.1 = (f32[768,128]{1,0:T(8,128)}, f32[384,128]{1,0:T(8,128)}, s32[16,512]{1,0:T(8,128)}) custom-call(s32[1]{0:T(128)} %bitcast.3.base_ref, f32[384,128]{1,0:T(8,128)} %bitcast.20, f32[384,128]{1,0:T(8,128)} %bitcast.21, f32[128,128]{1,0:T(8,128)} %refs_2_.1, s32[8,256]{1,0:T(8,128)} %bitcast.22, s32[8,256]{1,0:T(8,128)} %bitcast.23, ...), custom_call_target="tpu_custom_call" | custom-call | tf_op jit(solution)/shard_map/prep_sources/pallas_call | solution.py:268
  2.1 3.0 %collective-permute-start = (f32[384,128]{1,0:T(8,128)}, f32[384,128]{1,0:T(8,128)S(1)}, u32[]{:S(2)}, u32[]{:S(2)}) collective-permute-start(f32[384,128]{1,0:T(8,128)} %get-tuple-element.34), channel_id=1, source_target_pairs={{0,2},{1,3},{2,0},{3,1},{4,6},{5,7},{6,4},{7,5},{8,10},{9,11},{10,... | collective-permute-start | bytes 589832 | tf_op jit(solution)/shard_map/ppermute | solution.py:473
  5.1 0.0 collective-permute-start.2
  5.1 1.6 %collective-permute-start.4 = (f32[768,128]{1,0:T(8,128)}, f32[768,128]{1,0:T(8,128)S(1)}, u32[]{:S(2)}, u32[]{:S(2)}) collective-permute-start(f32[768,128]{1,0:T(8,128)} %get-tuple-element.37.refs_0_.refs_4_), channel_id=1, source_target_pairs={{0,4},{4,8},{8,12},{12,0},{1,5},{5,9},{9,13},{13,1},{2,6},{6,10},{... | collective-permute-start | bytes 1179656 | tf_op jit(solution)/shard_map/ppermute | solution.py:494
  6.7 2.2 %collective-permute-start.5 = (f32[768,128]{1,0:T(8,128)}, f32[768,128]{1,0:T(8,128)S(1)}, u32[]{:S(2)}, u32[]{:S(2)}) collective-permute-start(f32[768,128]{1,0:T(8,128)} %get-tuple-element.37.refs_0_.refs_4_), channel_id=1, source_target_pairs={{4,0},{8,4},{12,8},{0,12},{5,1},{9,5},{13,9},{1,13},{6,2},{10,6},{... | collective-permute-start | bytes 1179656 | tf_op jit(solution)/shard_map/ppermute | solution.py:495
  9.6 0.1 pad_add_fusion.facts_ref
  9.6 0.0 copy-start
  9.6 0.8 copy-done
  10.4 2.4 %index_work.1 = (s32[5,128]{1,0:T(8,128)S(1)}, s32[3,128]{1,0:T(4,128)S(1)}) custom-call(s32[4]{0:T(128)S(1)} %pad_add_fusion.facts_ref, s32[16,512]{1,0:T(8,128)S(1)} %copy-done), custom_call_target="tpu_custom_call" | custom-call | tf_op jit(solution)/shard_map/index_work/pallas_call | solution.py:381
  12.8 0.0 collective-permute-done.refs_2_
  12.8 0.1 collective-permute-start.3
  12.9 0.5 collective-permute-start.1
  13.4 0.9 %collective-permute-done.1.mate_list_ref = s32[5,128]{1,0:T(8,128)S(1)} collective-permute-done((s32[5,128]{1,0:T(8,128)S(1)}, s32[5,128]{1,0:T(8,128)S(1)}, u32[]{:S(2)}, u32[]{:S(2)}) %collective-permute-start.1) | collective-permute-done | bytes 2592 | tf_op jit(solution)/shard_map/ppermute | solution.py:473
  14.4 0.0 collective-permute-done.3.refs_3_
  14.4 0.0 collective-permute-done.2.refs_1_.refs_5_
  14.4 0.0 copy-start.1
  14.4 1.0 %copy-done.1 = f32[768,128]{1,0:T(8,128)S(1)} copy-done((f32[768,128]{1,0:T(8,128)S(1)}, f32[768,128]{1,0:T(8,128)}, u32[]{:S(2)}) %copy-start.1) | copy-done | bytes 393240
  15.4 7.9 %pairs_hop0.1 = (f32[2056,128]{1,0:T(8,128)S(1)}, f32[8,128]{1,0:T(8,128)S(1)}, f32[1536,128]{1,0:T(8,128)S(1)}) custom-call(s32[5,128]{1,0:T(8,128)S(1)} %get-tuple-element.36.list_ref, s32[5,128]{1,0:T(8,128)S(1)} %collective-permute-done.1.mate_list_ref, f32[768,128]{1,0:T(8,128)S(1)} %copy-done.1, f32[768,128]{1,0:T(8,128)S(1)} %collective-permute-done.2.refs_1_.refs_5_, ...), custom_call_target="tpu_custom_call" | custom-call | flops 1000000000 | bytes 1000000 | tf_op jit(solution)/shard_map/pairs_hop0/pallas_call | solution.py:210
  23.3 0.0 collective-permute-done.4.refs_3_
  23.3 3.3 %collective-permute-done.5.refs_4_ = f32[768,128]{1,0:T(8,128)S(1)} collective-permute-done((f32[768,128]{1,0:T(8,128)}, f32[768,128]{1,0:T(8,128)S(1)}, u32[]{:S(2)}, u32[]{:S(2)}) %collective-permute-start.5) | collective-permute-done | bytes 393248 | tf_op jit(solution)/shard_map/ppermute | solution.py:495
  26.6 0.0 collective-permute-start.7
  26.6 0.5 collective-permute-start.8
  27.1 1.2 %collective-permute-start.6 = (f32[768,128]{1,0:T(8,128)S(1)}, f32[768,128]{1,0:T(8,128)S(1)}, u32[]{:S(2)}, u32[]{:S(2)}) collective-permute-start(f32[768,128]{1,0:T(8,128)S(1)} %broadcast_select_fusion), channel_id=1, source_target_pairs={{0,4},{4,0},{8,12},{12,8},{1,5},{5,1},{9,13},{13,9},{2,6},{6,2},{1... | collective-permute-start | bytes 1179656 | tf_op jit(solution)/shard_map/ppermute | solution.py:517
  28.3 0.0 collective-permute-done.7.refs_5_
  28.3 0.5 collective-permute-done.8.refs_6_
  28.8 15.5 %pairs_hop1.1 = (f32[2056,128]{1,0:T(8,128)S(1)}, f32[8,128]{1,0:T(8,128)S(1)}) custom-call(s32[5,128]{1,0:T(8,128)S(1)} %get-tuple-element.36.list_ref, s32[5,128]{1,0:T(8,128)S(1)} %collective-permute-done.1.mate_list_ref, f32[1536,128]{1,0:T(8,128)S(1)} %get-tuple-element.39.refs_0_, ...), custom_call_target="tpu_custom_call", output_to_operand_aliasing={{0}: (4, {})} | custom-call | flops 8000000000 | bytes 1000000 | tf_op jit(solution)/shard_map/pairs_hop1/pallas_call | solution.py:210
  44.4 0.0 collective-permute-done.6.refs_3_
  44.4 0.2 collective-permute-start.9
  44.6 1.6 %collective-permute-done.9.refs_4_ = f32[768,128]{1,0:T(8,128)S(1)} collective-permute-done((f32[768,128]{1,0:T(8,128)S(1)}, f32[768,128]{1,0:T(8,128)S(1)}, u32[]{:S(2)}, u32[]{:S(2)}) %collective-permute-start.9) | collective-permute-done | bytes 393248 | tf_op jit(solution)/shard_map/ppermute | solution.py:473
  46.2 3.1 %pairs_hop2.1 = (f32[2056,128]{1,0:T(8,128)S(1)}, f32[8,128]{1,0:T(8,128)S(1)}, f32[384,128]{1,0:T(8,128)S(1)}, f32[384,128]{1,0:T(8,128)S(1)}) custom-call(s32[5,128]{1,0:T(8,128)S(1)} %get-tuple-element.36.list_ref, s32[5,128]{1,0:T(8,128)S(1)} %collective-permute-done.1.mate_list_ref, ...), custom_call_target="tpu_custom_call", output_to_operand_aliasing={{0}: (4, {})} | custom-call | flops 8000000000 | bytes 1000000 | tf_op jit(solution)/shard_map/pairs_hop2/pallas_call | solution.py:210
  49.3 0.2 collective-permute-start.10
  49.5 1.3 %collective-permute-done.10 = f32[384,128]{1,0:T(8,128)S(1)} collective-permute-done((f32[384,128]{1,0:T(8,128)S(1)}, f32[384,128]{1,0:T(8,128)S(1)}, u32[]{:S(2)}, u32[]{:S(2)}) %collective-permute-start.10) | collective-permute-done | bytes 196640 | tf_op jit(solution)/shard_map/ppermute | solution.py:473
  50.8 0.1 collective-permute-start.11
  50.9 8.2 %pairs_hop3.1 = (f32[2056,128]{1,0:T(8,128)S(1)}, f32[8,128]{1,0:T(8,128)}, f32[384,128]{1,0:T(8,128)S(1)}, f32[384,128]{1,0:T(8,128)S(1)}) custom-call(s32[5,128]{1,0:T(8,128)S(1)} %get-tuple-element.36.list_ref, s32[5,128]{1,0:T(8,128)S(1)} %collective-permute-done.1.mate_list_ref, ...), custom_call_target="tpu_custom_call", output_to_operand_aliasing={{0}: (4, {})} | custom-call | flops 8000000000 | bytes 1000000 | tf_op jit(solution)/shard_map/pairs_hop3/pallas_call | solution.py:210
  59.1 0.0 collective-permute-done.11.refs_2_
  59.1 0.1 collective-permute-start.12
  59.2 1.3 %collective-permute-done.12.refs_1_ = f32[384,128]{1,0:T(8,128)S(1)} collective-permute-done((f32[384,128]{1,0:T(8,128)S(1)}, f32[384,128]{1,0:T(8,128)S(1)}, u32[]{:S(2)}, u32[]{:S(2)}) %collective-permute-start.12) | collective-permute-done | bytes 196640 | tf_op jit(solution)/shard_map/ppermute | solution.py:473
  60.5 0.7 pack_owners.1
  61.3 14.8 %all_to_all.11 = f32[16,48,128]{2,1,0:T(8,128)S(1)} all-to-all(f32[16,48,128]{2,1,0:T(8,128)S(1)} %bitcast.19), channel_id=1, replica_groups=mesh['groups'=2,'row'=4,'col'=4] {'row','col'}, dimensions={0} | all-to-all | bytes 786432 | tf_op jit(solution)/shard_map/all_to_all | solution.py:542
  76.1 1.8 %unpack_drops.1 = f32[384,128]{1,0:T(8,128)} custom-call(s32[3,128]{1,0:T(4,128)S(1)} %get-tuple-element.33.place_ref, f32[768,128]{1,0:T(8,128)S(1)} %bitcast.18), custom_call_target="tpu_custom_call" | custom-call | tf_op jit(solution)/shard_map/unpack_drops/pallas_call | solution.py:439
  (2 shorter events, 0.1 us)
Async XLA Ops:
  2.1 10.8 %collective-permute-start = (f32[384,128]{1,0:T(8,128)}, f32[384,128]{1,0:T(8,128)S(1)}, u32[]{:S(2)}, u32[]{:S(2)}) collective-permute-start(f32[384,128]{1,0:T(8,128)} %get-tuple-element.34), channel_id=1, source_target_pairs={{0,2},{1,3},{2,0},{3,1},{4,6},{5,7},{6,4},{7,5},{8,10},{9,11},{10,... | collective-permute-start | bytes 589832 | tf_op jit(solution)/shard_map/ppermute | solution.py:473
  5.1 9.3 %collective-permute-start.2 = (f32[768,128]{1,0:T(8,128)}, f32[768,128]{1,0:T(8,128)S(1)}, u32[]{:S(2)}, u32[]{:S(2)}) collective-permute-start(f32[768,128]{1,0:T(8,128)} %get-tuple-element.37.refs_0_.refs_4_), channel_id=1, source_target_pairs={{0,1},{1,0},{2,3},{3,2},{4,5},{5,4},{6,7},{7,6},{8,9},{9,8},{10,11... | collective-permute-start | bytes 1179656 | tf_op jit(solution)/shard_map/ppermute | solution.py:473
  5.1 18.2 %collective-permute-start.4 = (f32[768,128]{1,0:T(8,128)}, f32[768,128]{1,0:T(8,128)S(1)}, u32[]{:S(2)}, u32[]{:S(2)}) collective-permute-start(f32[768,128]{1,0:T(8,128)} %get-tuple-element.37.refs_0_.refs_4_), channel_id=1, source_target_pairs={{0,4},{4,8},{8,12},{12,0},{1,5},{5,9},{9,13},{13,1},{2,6},{6,10},{... | collective-permute-start | bytes 1179656 | tf_op jit(solution)/shard_map/ppermute | solution.py:494
  6.7 19.9 %collective-permute-start.5 = (f32[768,128]{1,0:T(8,128)}, f32[768,128]{1,0:T(8,128)S(1)}, u32[]{:S(2)}, u32[]{:S(2)}) collective-permute-start(f32[768,128]{1,0:T(8,128)} %get-tuple-element.37.refs_0_.refs_4_), channel_id=1, source_target_pairs={{4,0},{8,4},{12,8},{0,12},{5,1},{9,5},{13,9},{1,13},{6,2},{10,6},{... | collective-permute-start | bytes 1179656 | tf_op jit(solution)/shard_map/ppermute | solution.py:495
  9.6 0.8 copy-start
  12.8 1.5 %collective-permute-start.3 = (f32[384,128]{1,0:T(8,128)S(1)}, f32[384,128]{1,0:T(8,128)S(1)}, u32[]{:S(2)}, u32[]{:S(2)}) collective-permute-start(f32[384,128]{1,0:T(8,128)S(1)} %collective-permute-done.refs_2_), channel_id=1, source_target_pairs={{0,1},{1,0},{2,3},{3,2},{4,5},{5,4},{6,7},{7,6},{8,9},{9,8},{10,11... | collective-permute-start | bytes 589832 | tf_op jit(solution)/shard_map/ppermute | solution.py:473
  12.9 1.4 %collective-permute-start.1 = (s32[5,128]{1,0:T(8,128)S(1)}, s32[5,128]{1,0:T(8,128)S(1)}, u32[]{:S(2)}, u32[]{:S(2)}) collective-permute-start(s32[5,128]{1,0:T(8,128)S(1)} %get-tuple-element.36.list_ref), channel_id=1, source_target_pairs={{0,1},{1,0},{2,3},{3,2},{4,5},{5,4},{6,7},{7,6},{8,9},{9,8},{10,11... | collective-permute-start | bytes 7688 | tf_op jit(solution)/shard_map/ppermute | solution.py:473
  14.4 1.0 %copy-start.1 = (f32[768,128]{1,0:T(8,128)S(1)}, f32[768,128]{1,0:T(8,128)}, u32[]{:S(2)}) copy-start(f32[768,128]{1,0:T(8,128)} %get-tuple-element.37.refs_0_.refs_4_) | copy-start | bytes 1179652
  26.6 1.8 %collective-permute-start.7 = (f32[768,128]{1,0:T(8,128)S(1)}, f32[768,128]{1,0:T(8,128)S(1)}, u32[]{:S(2)}, u32[]{:S(2)}) collective-permute-start(f32[768,128]{1,0:T(8,128)S(1)} %collective-permute-done.4.refs_3_), channel_id=1, source_target_pairs={{0,1},{1,0},{2,3},{3,2},{4,5},{5,4},{6,7},{7,6},{8,9},{9,8},{10,11... | collective-permute-start | bytes 1179656 | tf_op jit(solution)/shard_map/ppermute | solution.py:473
  26.6 2.3 %collective-permute-start.8 = (f32[768,128]{1,0:T(8,128)S(1)}, f32[768,128]{1,0:T(8,128)S(1)}, u32[]{:S(2)}, u32[]{:S(2)}) collective-permute-start(f32[768,128]{1,0:T(8,128)S(1)} %collective-permute-done.5.refs_4_), channel_id=1, source_target_pairs={{0,1},{1,0},{2,3},{3,2},{4,5},{5,4},{6,7},{7,6},{8,9},{9,8},{10,11... | collective-permute-start | bytes 1179656 | tf_op jit(solution)/shard_map/ppermute | solution.py:473
  27.1 17.3 %collective-permute-start.6 = (f32[768,128]{1,0:T(8,128)S(1)}, f32[768,128]{1,0:T(8,128)S(1)}, u32[]{:S(2)}, u32[]{:S(2)}) collective-permute-start(f32[768,128]{1,0:T(8,128)S(1)} %broadcast_select_fusion), channel_id=1, source_target_pairs={{0,4},{4,0},{8,12},{12,8},{1,5},{5,1},{9,13},{13,9},{2,6},{6,2},{1... | collective-permute-start | bytes 1179656 | tf_op jit(solution)/shard_map/ppermute | solution.py:517
  44.4 1.8 %collective-permute-start.9 = (f32[768,128]{1,0:T(8,128)S(1)}, f32[768,128]{1,0:T(8,128)S(1)}, u32[]{:S(2)}, u32[]{:S(2)}) collective-permute-start(f32[768,128]{1,0:T(8,128)S(1)} %collective-permute-done.6.refs_3_), channel_id=1, source_target_pairs={{0,1},{1,0},{2,3},{3,2},{4,5},{5,4},{6,7},{7,6},{8,9},{9,8},{10,11... | collective-permute-start | bytes 1179656 | tf_op jit(solution)/shard_map/ppermute | solution.py:473
  49.3 1.5 %collective-permute-start.10 = (f32[384,128]{1,0:T(8,128)S(1)}, f32[384,128]{1,0:T(8,128)S(1)}, u32[]{:S(2)}, u32[]{:S(2)}) collective-permute-start(f32[384,128]{1,0:T(8,128)S(1)} %get-tuple-element.50), channel_id=1, source_target_pairs={{0,1},{1,0},{2,3},{3,2},{4,5},{5,4},{6,7},{7,6},{8,9},{9,8},{10,11... | collective-permute-start | bytes 589832 | tf_op jit(solution)/shard_map/ppermute | solution.py:473
  50.8 8.3 %collective-permute-start.11 = (f32[384,128]{1,0:T(8,128)S(1)}, f32[384,128]{1,0:T(8,128)S(1)}, u32[]{:S(2)}, u32[]{:S(2)}) collective-permute-start(f32[384,128]{1,0:T(8,128)S(1)} %add.12), channel_id=1, source_target_pairs={{0,2},{1,3},{2,0},{3,1},{4,6},{5,7},{6,4},{7,5},{8,10},{9,11},{10,... | collective-permute-start | bytes 589832 | tf_op jit(solution)/shard_map/ppermute | solution.py:473
  59.1 1.4 %collective-permute-start.12 = (f32[384,128]{1,0:T(8,128)S(1)}, f32[384,128]{1,0:T(8,128)S(1)}, u32[]{:S(2)}, u32[]{:S(2)}) collective-permute-start(f32[384,128]{1,0:T(8,128)S(1)} %get-tuple-element.57), channel_id=1, source_target_pairs={{0,1},{1,0},{2,3},{3,2},{4,5},{5,4},{6,7},{7,6},{8,9},{9,8},{10,11... | collective-permute-start | bytes 589832 | tf_op jit(solution)/shard_map/ppermute | solution.py:473
where the time goes:
time: 77.1 us; the launch traced here: 77.8 us
  Pallas kernels  41.7 us (54%)
  blocking collectives  14.8 us (19%)
  starting transfers between devices  9.69 us (13%)
  waiting for transfers between devices  8.97 us (12%)
  local copies, waits for them, and re-layouts  1.75 us (2%)
    pallas_call x4, Pallas kernels, hop_call(): pl.pallas_call(functools.partial(hop_kernel, spec), out_shape=out_shape,...  34.7 us
    all_to_all x1, blocking collectives, per_device(): lax.all_to_all(outgoing, ('row', 'col'), split_axis=0, concat_axis=0, til...  14.8 us
    ppermute x10, waiting for transfers between devices, swap(): return lax.ppermute(value, 'col', [(c, c ^ bit) for c in range(cols)])  5.71 us
    ppermute x10, starting transfers between devices, swap(): return lax.ppermute(value, 'col', [(c, c ^ bit) for c in range(cols)])  4.67 us
    ppermute x1, waiting for transfers between devices, per_device(): left = lax.ppermute(block, 'row', to_left)  3.26 us
    pallas_call x1, Pallas kernels, index_call(): pl.pallas_call(functools.partial(index_kernel, spec), out_shape=[jax.Shap...  2.43 us
    ppermute x1, starting transfers between devices, per_device(): left = lax.ppermute(block, 'row', to_left)  2.25 us
    pallas_call x1, Pallas kernels, prep_call(): pl.pallas_call(functools.partial(prep_kernel, n), out_shape=[jax.ShapeDty...  2.07 us
  transfers between devices with their start and end apart: 13, of which 6 were waited for; matrix products, arithmetic and copies ran while one was open for 0% of the time, Pallas kernels for 44%

commit v1 on v0

--- a/solution.py
+++ b/solution.py
@@ -126,11 +126,11 @@
     def wide(value):
         return jnp.broadcast_to(value, (8, slots))
 
-    def run(level):
+    def run(level, until):
         groups = slots // 8 * (levels - level) // levels
-        lane = hop * levels + level
-        own_start, own_end = list_ref[bound_row, lane], list_ref[bound_row, lane + 1]
-        mate_start, mate_end = mate_list_ref[bound_row, lane], mate_list_ref[bound_row, lane + 1]
+        lane, end = hop * levels + level, hop * levels + until
+        own_start, own_end = list_ref[bound_row, lane], list_ref[bound_row, end]
+        mate_start, mate_end = mate_list_ref[bound_row, lane], mate_list_ref[bound_row, end]
         own_count = (own_end - own_start + 1) >> 1
         count = own_count + ((mate_end - mate_start) >> 1)
         after_own = mate_start + 1 - 2 * own_count
@@ -176,8 +176,11 @@
 
         lax.fori_loop(0, (count + unroll - 1) // unroll, step, 0)
 
-    for level in range(levels):
-        run(level)
+    if emit:
+        run(0, levels)
+    else:
+        for level in range(levels):
+            run(level, level + 1)
     for out_ref, out_homes in zip(out_refs if emit else [], emit):
         for place, h in enumerate(out_homes):
 
@@ -230,15 +233,12 @@
 def prep_kernel(n, base_ref, *refs):
     ins, (out_ref, own_ref, small_ref), held, sems = refs[:8], refs[8:11], refs[11:19], refs[19]
     copies = [pltpu.make_async_copy(a, b, sems.at[k]) for k, (a, b) in enumerate(zip(ins, held))]
-    for copy in copies:
+    for copy in copies[3:5] + copies[:3] + copies[5:]:
         copy.start()
-    for copy in copies:
-        copy.wait()
     position_ref, normal_ref, curvature_ref, cluster_ref, count_ref, owner_ref, target_ref, source_ref = held
     slots = position_ref.shape[1]
-    scaled = position_ref[...] * length_scale
-    out_ref[: 3 * n, :] = scaled
-    own_ref[...] = scaled
+    for copy in copies[3:5]:
+        copy.wait()
     mine = base_ref[0] + lax.broadcasted_iota(i32, (n, 128), 0)
     total = jnp.zeros((n, 128), f32)
     for k in range(cluster_ref.shape[0]):
@@ -248,6 +248,11 @@
             count = jnp.broadcast_to(count_ref[k : k + 1, part].astype(f32), (n, 128))
             total = total + jnp.where(cluster == mine, count, 0.0)
     live_count = jnp.sum(total, axis=1, keepdims=True)
+    for copy in copies[:3] + copies[5:]:
+        copy.wait()
+    scaled = position_ref[...] * length_scale
+    out_ref[: 3 * n, :] = scaled
+    own_ref[...] = scaled
     lane = lax.broadcasted_iota(i32, (n, slots), 1).astype(f32)
     strength = jnp.where(lane < live_count, curvature_ref[...] * force_scale, 0.0)
     for k in range(3):

time: 77.1 us -> 76.2 us (0.988)
  Pallas kernels: 41.7 us -> 24.8 us
  blocking collectives: 14.8 us -> 22.3 us
  waiting for transfers between devices: 8.97 us -> 16.1 us
  starting transfers between devices: 9.69 us -> 10.6 us
    pallas_call x4, Pallas kernels: 34.7 us -> 17.9 us  [hop_call(): pl.pallas_call(functools.partial(hop_kernel, spec), out_shape=out_shape,...]
    all_to_all x1, blocking collectives: 14.8 us -> 22.3 us  [per_device(): lax.all_to_all(outgoing, ('row', 'col'), split_axis=0, concat_axis=0, til...]
    ppermute x1, waiting for transfers between devices: 3.26 us -> 7.09 us  [per_device(): left = lax.ppermute(block, 'row', to_left)]
    ppermute x1, waiting for transfers between devices: 0.01 us -> 2.41 us  [per_device(): opposite = [lax.ppermute(passed, 'row', [(0, 1), (1, 0), (2, 3), (3, 2)])]]
    ppermute x10, waiting for transfers between devices: 5.71 us -> 6.62 us  [swap(): return lax.ppermute(value, 'col', [(c, c ^ bit) for c in range(cols)])]
    ppermute x10, starting transfers between devices: 4.67 us -> 5.55 us  [swap(): return lax.ppermute(value, 'col', [(c, c ^ bit) for c in range(cols)])]
  transfers between devices with their start and end apart: 13 -> 13, of which waited for: 6 -> 8; matrix products, arithmetic and copies ran while one was open for 0% -> 0% of each run, Pallas kernels for 44% -> 24%
where the time goes in v1:
time: 76.2 us; the launch traced here: 76.4 us
  Pallas kernels  24.8 us (33%)
  blocking collectives  22.3 us (29%)
  waiting for transfers between devices  16.1 us (21%)
  starting transfers between devices  10.6 us (14%)
  local copies, waits for them, and re-layouts  1.75 us (2%)
    all_to_all x1, blocking collectives, per_device(): lax.all_to_all(outgoing, ('row', 'col'), split_axis=0, concat_axis=0, til...  22.3 us
    pallas_call x4, Pallas kernels, hop_call(): pl.pallas_call(functools.partial(hop_kernel, spec), out_shape=out_shape,...  17.9 us
    ppermute x1, waiting for transfers between devices, per_device(): left = lax.ppermute(block, 'row', to_left)  7.09 us
    ppermute x10, waiting for transfers between devices, swap(): return lax.ppermute(value, 'col', [(c, c ^ bit) for c in range(cols)])  6.62 us
    ppermute x10, starting transfers between devices, swap(): return lax.ppermute(value, 'col', [(c, c ^ bit) for c in range(cols)])  5.55 us
    pallas_call x1, Pallas kernels, index_call(): pl.pallas_call(functools.partial(index_kernel, spec), out_shape=[jax.Shap...  2.43 us
    ppermute x1, waiting for transfers between devices, per_device(): opposite = [lax.ppermute(passed, 'row', [(0, 1), (1, 0), (2, 3), (3, 2)])]  2.41 us
    ppermute x1, starting transfers between devices, per_device(): left = lax.ppermute(block, 'row', to_left)  2.25 us
  transfers between devices with their start and end apart: 13, of which 8 were waited for; matrix products, arithmetic and copies ran while one was open for 0% of the time, Pallas kernels for 24%

profile of v1, /device:TPU:0, one launch (start us, length us, event | category | flops | bytes accessed | tf_op | source)
XLA Modules:
  0.0 76.4 jit_solution(7716758780760930786)
XLA Ops:
  0.0 2.0 %prep_sources.1 = (f32[768,128]{1,0:T(8,128)}, f32[384,128]{1,0:T(8,128)}, s32[16,512]{1,0:T(8,128)}) custom-call(s32[1]{0:T(128)} %bitcast.3.base_ref, f32[384,128]{1,0:T(8,128)} %bitcast.20, f32[384,128]{1,0:T(8,128)} %bitcast.21, f32[128,128]{1,0:T(8,128)} %refs_2_.1, s32[8,256]{1,0:T(8,128)} %bitcast.22, s32[8,256]{1,0:T(8,128)} %bitcast.23, ...), custom_call_target="tpu_custom_call" | custom-call | tf_op jit(solution)/shard_map/prep_sources/pallas_call | solution.py:273
  2.0 3.0 %collective-permute-start = (f32[384,128]{1,0:T(8,128)}, f32[384,128]{1,0:T(8,128)S(1)}, u32[]{:S(2)}, u32[]{:S(2)}) collective-permute-start(f32[384,128]{1,0:T(8,128)} %get-tuple-element.34), channel_id=1, source_target_pairs={{0,2},{1,3},{2,0},{3,1},{4,6},{5,7},{6,4},{7,5},{8,10},{9,11},{10,... | collective-permute-start | bytes 589832 | tf_op jit(solution)/shard_map/ppermute | solution.py:478
  5.0 0.0 collective-permute-start.2
  5.0 1.6 %collective-permute-start.4 = (f32[768,128]{1,0:T(8,128)}, f32[768,128]{1,0:T(8,128)S(1)}, u32[]{:S(2)}, u32[]{:S(2)}) collective-permute-start(f32[768,128]{1,0:T(8,128)} %get-tuple-element.37.refs_0_.refs_4_), channel_id=1, source_target_pairs={{0,4},{4,8},{8,12},{12,0},{1,5},{5,9},{9,13},{13,1},{2,6},{6,10},{... | collective-permute-start | bytes 1179656 | tf_op jit(solution)/shard_map/ppermute | solution.py:499
  6.6 2.2 %collective-permute-start.5 = (f32[768,128]{1,0:T(8,128)}, f32[768,128]{1,0:T(8,128)S(1)}, u32[]{:S(2)}, u32[]{:S(2)}) collective-permute-start(f32[768,128]{1,0:T(8,128)} %get-tuple-element.37.refs_0_.refs_4_), channel_id=1, source_target_pairs={{4,0},{8,4},{12,8},{0,12},{5,1},{9,5},{13,9},{1,13},{6,2},{10,6},{... | collective-permute-start | bytes 1179656 | tf_op jit(solution)/shard_map/ppermute | solution.py:500
  9.5 0.1 pad_add_fusion.facts_ref
  9.5 0.0 copy-start
  9.6 0.8 copy-done
  10.3 2.4 %index_work.1 = (s32[5,128]{1,0:T(8,128)S(1)}, s32[3,128]{1,0:T(4,128)S(1)}) custom-call(s32[4]{0:T(128)S(1)} %pad_add_fusion.facts_ref, s32[16,512]{1,0:T(8,128)S(1)} %copy-done), custom_call_target="tpu_custom_call" | custom-call | tf_op jit(solution)/shard_map/index_work/pallas_call | solution.py:386
  12.7 0.0 collective-permute-done.refs_2_
  12.7 0.1 collective-permute-start.3
  12.8 0.5 collective-permute-start.1
  13.3 0.9 %collective-permute-done.1.mate_list_ref = s32[5,128]{1,0:T(8,128)S(1)} collective-permute-done((s32[5,128]{1,0:T(8,128)S(1)}, s32[5,128]{1,0:T(8,128)S(1)}, u32[]{:S(2)}, u32[]{:S(2)}) %collective-permute-start.1) | collective-permute-done | bytes 2592 | tf_op jit(solution)/shard_map/ppermute | solution.py:478
  14.3 0.0 collective-permute-done.3.refs_3_
  14.3 0.0 collective-permute-done.2.refs_1_.refs_5_
  14.3 0.0 copy-start.1
  14.3 1.0 %copy-done.1 = f32[768,128]{1,0:T(8,128)S(1)} copy-done((f32[768,128]{1,0:T(8,128)S(1)}, f32[768,128]{1,0:T(8,128)}, u32[]{:S(2)}) %copy-start.1) | copy-done | bytes 393240
  15.3 4.1 %pairs_hop0.1 = (f32[2056,128]{1,0:T(8,128)S(1)}, f32[8,128]{1,0:T(8,128)S(1)}, f32[1536,128]{1,0:T(8,128)S(1)}) custom-call(s32[5,128]{1,0:T(8,128)S(1)} %get-tuple-element.36.list_ref, s32[5,128]{1,0:T(8,128)S(1)} %collective-permute-done.1.mate_list_ref, f32[768,128]{1,0:T(8,128)S(1)} %copy-done.1, f32[768,128]{1,0:T(8,128)S(1)} %collective-permute-done.2.refs_1_.refs_5_, ...), custom_call_target="tpu_custom_call" | custom-call | flops 1000000000 | bytes 1000000 | tf_op jit(solution)/shard_map/pairs_hop0/pallas_call | solution.py:213
  19.4 0.0 collective-permute-done.4.refs_3_
  19.4 7.1 %collective-permute-done.5.refs_4_ = f32[768,128]{1,0:T(8,128)S(1)} collective-permute-done((f32[768,128]{1,0:T(8,128)}, f32[768,128]{1,0:T(8,128)S(1)}, u32[]{:S(2)}, u32[]{:S(2)}) %collective-permute-start.5) | collective-permute-done | bytes 393248 | tf_op jit(solution)/shard_map/ppermute | solution.py:500
  26.5 0.0 collective-permute-start.7
  26.5 0.5 collective-permute-start.8
  27.0 1.2 %collective-permute-start.6 = (f32[768,128]{1,0:T(8,128)S(1)}, f32[768,128]{1,0:T(8,128)S(1)}, u32[]{:S(2)}, u32[]{:S(2)}) collective-permute-start(f32[768,128]{1,0:T(8,128)S(1)} %broadcast_select_fusion), channel_id=1, source_target_pairs={{0,4},{4,0},{8,12},{12,8},{1,5},{5,1},{9,13},{13,9},{2,6},{6,2},{1... | collective-permute-start | bytes 1179656 | tf_op jit(solution)/shard_map/ppermute | solution.py:522
  28.2 0.0 collective-permute-done.7.refs_5_
  28.2 0.5 collective-permute-done.8.refs_6_
  28.7 6.9 %pairs_hop1.1 = (f32[2056,128]{1,0:T(8,128)S(1)}, f32[8,128]{1,0:T(8,128)S(1)}) custom-call(s32[5,128]{1,0:T(8,128)S(1)} %get-tuple-element.36.list_ref, s32[5,128]{1,0:T(8,128)S(1)} %collective-permute-done.1.mate_list_ref, f32[1536,128]{1,0:T(8,128)S(1)} %get-tuple-element.39.refs_0_, ...), custom_call_target="tpu_custom_call", output_to_operand_aliasing={{0}: (4, {})} | custom-call | flops 8000000000 | bytes 1000000 | tf_op jit(solution)/shard_map/pairs_hop1/pallas_call | solution.py:213
  35.7 2.4 %collective-permute-done.6.refs_3_ = f32[768,128]{1,0:T(8,128)S(1)} collective-permute-done((f32[768,128]{1,0:T(8,128)S(1)}, f32[768,128]{1,0:T(8,128)S(1)}, u32[]{:S(2)}, u32[]{:S(2)}) %collective-permute-start.6) | collective-permute-done | bytes 393248 | tf_op jit(solution)/shard_map/ppermute | solution.py:522
  38.1 0.0 collective-permute-start.9
  38.1 1.7 %collective-permute-done.9.refs_4_ = f32[768,128]{1,0:T(8,128)S(1)} collective-permute-done((f32[768,128]{1,0:T(8,128)S(1)}, f32[768,128]{1,0:T(8,128)S(1)}, u32[]{:S(2)}, u32[]{:S(2)}) %collective-permute-start.9) | collective-permute-done | bytes 393248 | tf_op jit(solution)/shard_map/ppermute | solution.py:478
  39.8 1.8 %pairs_hop2.1 = (f32[2056,128]{1,0:T(8,128)S(1)}, f32[8,128]{1,0:T(8,128)S(1)}, f32[384,128]{1,0:T(8,128)S(1)}, f32[384,128]{1,0:T(8,128)S(1)}) custom-call(s32[5,128]{1,0:T(8,128)S(1)} %get-tuple-element.36.list_ref, s32[5,128]{1,0:T(8,128)S(1)} %collective-permute-done.1.mate_list_ref, ...), custom_call_target="tpu_custom_call", output_to_operand_aliasing={{0}: (4, {})} | custom-call | flops 8000000000 | bytes 1000000 | tf_op jit(solution)/shard_map/pairs_hop2/pallas_call | solution.py:213
  41.6 0.2 collective-permute-start.10
  41.8 1.3 %collective-permute-done.10 = f32[384,128]{1,0:T(8,128)S(1)} collective-permute-done((f32[384,128]{1,0:T(8,128)S(1)}, f32[384,128]{1,0:T(8,128)S(1)}, u32[]{:S(2)}, u32[]{:S(2)}) %collective-permute-start.10) | collective-permute-done | bytes 196640 | tf_op jit(solution)/shard_map/ppermute | solution.py:478
  43.2 1.3 %collective-permute-start.11 = (f32[384,128]{1,0:T(8,128)S(1)}, f32[384,128]{1,0:T(8,128)S(1)}, u32[]{:S(2)}, u32[]{:S(2)}) collective-permute-start(f32[384,128]{1,0:T(8,128)S(1)} %add.12), channel_id=1, source_target_pairs={{0,2},{1,3},{2,0},{3,1},{4,6},{5,7},{6,4},{7,5},{8,10},{9,11},{10,... | collective-permute-start | bytes 589832 | tf_op jit(solution)/shard_map/ppermute | solution.py:478
  44.4 5.1 %pairs_hop3.1 = (f32[2056,128]{1,0:T(8,128)S(1)}, f32[8,128]{1,0:T(8,128)}, f32[384,128]{1,0:T(8,128)S(1)}, f32[384,128]{1,0:T(8,128)S(1)}) custom-call(s32[5,128]{1,0:T(8,128)S(1)} %get-tuple-element.36.list_ref, s32[5,128]{1,0:T(8,128)S(1)} %collective-permute-done.1.mate_list_ref, ...), custom_call_target="tpu_custom_call", output_to_operand_aliasing={{0}: (4, {})} | custom-call | flops 8000000000 | bytes 1000000 | tf_op jit(solution)/shard_map/pairs_hop3/pallas_call | solution.py:213
  49.5 0.7 collective-permute-done.11.refs_2_
  50.2 0.0 collective-permute-start.12
  50.2 1.4 %collective-permute-done.12.refs_1_ = f32[384,128]{1,0:T(8,128)S(1)} collective-permute-done((f32[384,128]{1,0:T(8,128)S(1)}, f32[384,128]{1,0:T(8,128)S(1)}, u32[]{:S(2)}, u32[]{:S(2)}) %collective-permute-start.12) | collective-permute-done | bytes 196640 | tf_op jit(solution)/shard_map/ppermute | solution.py:478
  51.6 0.7 pack_owners.1
  52.4 22.3 %all_to_all.11 = f32[16,48,128]{2,1,0:T(8,128)S(1)} all-to-all(f32[16,48,128]{2,1,0:T(8,128)S(1)} %bitcast.19), channel_id=1, replica_groups=mesh['groups'=2,'row'=4,'col'=4] {'row','col'}, dimensions={0} | all-to-all | bytes 786432 | tf_op jit(solution)/shard_map/all_to_all | solution.py:547
  74.7 1.8 %unpack_drops.1 = f32[384,128]{1,0:T(8,128)} custom-call(s32[3,128]{1,0:T(4,128)S(1)} %get-tuple-element.33.place_ref, f32[768,128]{1,0:T(8,128)S(1)} %bitcast.18), custom_call_target="tpu_custom_call" | custom-call | tf_op jit(solution)/shard_map/unpack_drops/pallas_call | solution.py:444
  (2 shorter events, 0.1 us)
Async XLA Ops:
  2.0 10.8 %collective-permute-start = (f32[384,128]{1,0:T(8,128)}, f32[384,128]{1,0:T(8,128)S(1)}, u32[]{:S(2)}, u32[]{:S(2)}) collective-permute-start(f32[384,128]{1,0:T(8,128)} %get-tuple-element.34), channel_id=1, source_target_pairs={{0,2},{1,3},{2,0},{3,1},{4,6},{5,7},{6,4},{7,5},{8,10},{9,11},{10,... | collective-permute-start | bytes 589832 | tf_op jit(solution)/shard_map/ppermute | solution.py:478
  5.0 9.3 %collective-permute-start.2 = (f32[768,128]{1,0:T(8,128)}, f32[768,128]{1,0:T(8,128)S(1)}, u32[]{:S(2)}, u32[]{:S(2)}) collective-permute-start(f32[768,128]{1,0:T(8,128)} %get-tuple-element.37.refs_0_.refs_4_), channel_id=1, source_target_pairs={{0,1},{1,0},{2,3},{3,2},{4,5},{5,4},{6,7},{7,6},{8,9},{9,8},{10,11... | collective-permute-start | bytes 1179656 | tf_op jit(solution)/shard_map/ppermute | solution.py:478
  5.0 14.4 %collective-permute-start.4 = (f32[768,128]{1,0:T(8,128)}, f32[768,128]{1,0:T(8,128)S(1)}, u32[]{:S(2)}, u32[]{:S(2)}) collective-permute-start(f32[768,128]{1,0:T(8,128)} %get-tuple-element.37.refs_0_.refs_4_), channel_id=1, source_target_pairs={{0,4},{4,8},{8,12},{12,0},{1,5},{5,9},{9,13},{13,1},{2,6},{6,10},{... | collective-permute-start | bytes 1179656 | tf_op jit(solution)/shard_map/ppermute | solution.py:499
  6.6 19.9 %collective-permute-start.5 = (f32[768,128]{1,0:T(8,128)}, f32[768,128]{1,0:T(8,128)S(1)}, u32[]{:S(2)}, u32[]{:S(2)}) collective-permute-start(f32[768,128]{1,0:T(8,128)} %get-tuple-element.37.refs_0_.refs_4_), channel_id=1, source_target_pairs={{4,0},{8,4},{12,8},{0,12},{5,1},{9,5},{13,9},{1,13},{6,2},{10,6},{... | collective-permute-start | bytes 1179656 | tf_op jit(solution)/shard_map/ppermute | solution.py:500
  9.5 0.8 copy-start
  12.7 1.5 %collective-permute-start.3 = (f32[384,128]{1,0:T(8,128)S(1)}, f32[384,128]{1,0:T(8,128)S(1)}, u32[]{:S(2)}, u32[]{:S(2)}) collective-permute-start(f32[384,128]{1,0:T(8,128)S(1)} %collective-permute-done.refs_2_), channel_id=1, source_target_pairs={{0,1},{1,0},{2,3},{3,2},{4,5},{5,4},{6,7},{7,6},{8,9},{9,8},{10,11... | collective-permute-start | bytes 589832 | tf_op jit(solution)/shard_map/ppermute | solution.py:478
  12.8 1.4 %collective-permute-start.1 = (s32[5,128]{1,0:T(8,128)S(1)}, s32[5,128]{1,0:T(8,128)S(1)}, u32[]{:S(2)}, u32[]{:S(2)}) collective-permute-start(s32[5,128]{1,0:T(8,128)S(1)} %get-tuple-element.36.list_ref), channel_id=1, source_target_pairs={{0,1},{1,0},{2,3},{3,2},{4,5},{5,4},{6,7},{7,6},{8,9},{9,8},{10,11... | collective-permute-start | bytes 7688 | tf_op jit(solution)/shard_map/ppermute | solution.py:478
  14.3 1.0 %copy-start.1 = (f32[768,128]{1,0:T(8,128)S(1)}, f32[768,128]{1,0:T(8,128)}, u32[]{:S(2)}) copy-start(f32[768,128]{1,0:T(8,128)} %get-tuple-element.37.refs_0_.refs_4_) | copy-start | bytes 1179652
  26.5 1.8 %collective-permute-start.7 = (f32[768,128]{1,0:T(8,128)S(1)}, f32[768,128]{1,0:T(8,128)S(1)}, u32[]{:S(2)}, u32[]{:S(2)}) collective-permute-start(f32[768,128]{1,0:T(8,128)S(1)} %collective-permute-done.4.refs_3_), channel_id=1, source_target_pairs={{0,1},{1,0},{2,3},{3,2},{4,5},{5,4},{6,7},{7,6},{8,9},{9,8},{10,11... | collective-permute-start | bytes 1179656 | tf_op jit(solution)/shard_map/ppermute | solution.py:478
  26.5 2.3 %collective-permute-start.8 = (f32[768,128]{1,0:T(8,128)S(1)}, f32[768,128]{1,0:T(8,128)S(1)}, u32[]{:S(2)}, u32[]{:S(2)}) collective-permute-start(f32[768,128]{1,0:T(8,128)S(1)} %collective-permute-done.5.refs_4_), channel_id=1, source_target_pairs={{0,1},{1,0},{2,3},{3,2},{4,5},{5,4},{6,7},{7,6},{8,9},{9,8},{10,11... | collective-permute-start | bytes 1179656 | tf_op jit(solution)/shard_map/ppermute | solution.py:478
  27.0 11.1 %collective-permute-start.6 = (f32[768,128]{1,0:T(8,128)S(1)}, f32[768,128]{1,0:T(8,128)S(1)}, u32[]{:S(2)}, u32[]{:S(2)}) collective-permute-start(f32[768,128]{1,0:T(8,128)S(1)} %broadcast_select_fusion), channel_id=1, source_target_pairs={{0,4},{4,0},{8,12},{12,8},{1,5},{5,1},{9,13},{13,9},{2,6},{6,2},{1... | collective-permute-start | bytes 1179656 | tf_op jit(solution)/shard_map/ppermute | solution.py:522
  38.1 1.7 %collective-permute-start.9 = (f32[768,128]{1,0:T(8,128)S(1)}, f32[768,128]{1,0:T(8,128)S(1)}, u32[]{:S(2)}, u32[]{:S(2)}) collective-permute-start(f32[768,128]{1,0:T(8,128)S(1)} %collective-permute-done.6.refs_3_), channel_id=1, source_target_pairs={{0,1},{1,0},{2,3},{3,2},{4,5},{5,4},{6,7},{7,6},{8,9},{9,8},{10,11... | collective-permute-start | bytes 1179656 | tf_op jit(solution)/shard_map/ppermute | solution.py:478
  41.6 1.5 %collective-permute-start.10 = (f32[384,128]{1,0:T(8,128)S(1)}, f32[384,128]{1,0:T(8,128)S(1)}, u32[]{:S(2)}, u32[]{:S(2)}) collective-permute-start(f32[384,128]{1,0:T(8,128)S(1)} %get-tuple-element.50), channel_id=1, source_target_pairs={{0,1},{1,0},{2,3},{3,2},{4,5},{5,4},{6,7},{7,6},{8,9},{9,8},{10,11... | collective-permute-start | bytes 589832 | tf_op jit(solution)/shard_map/ppermute | solution.py:478
  43.2 7.0 %collective-permute-start.11 = (f32[384,128]{1,0:T(8,128)S(1)}, f32[384,128]{1,0:T(8,128)S(1)}, u32[]{:S(2)}, u32[]{:S(2)}) collective-permute-start(f32[384,128]{1,0:T(8,128)S(1)} %add.12), channel_id=1, source_target_pairs={{0,2},{1,3},{2,0},{3,1},{4,6},{5,7},{6,4},{7,5},{8,10},{9,11},{10,... | collective-permute-start | bytes 589832 | tf_op jit(solution)/shard_map/ppermute | solution.py:478
  50.2 1.4 %collective-permute-start.12 = (f32[384,128]{1,0:T(8,128)S(1)}, f32[384,128]{1,0:T(8,128)S(1)}, u32[]{:S(2)}, u32[]{:S(2)}) collective-permute-start(f32[384,128]{1,0:T(8,128)S(1)} %get-tuple-element.57), channel_id=1, source_target_pairs={{0,1},{1,0},{2,3},{3,2},{4,5},{5,4},{6,7},{7,6},{8,9},{9,8},{10,11... | collective-permute-start | bytes 589832 | tf_op jit(solution)/shard_map/ppermute | solution.py:478
